TPU v7x, 512 devices: a whole 4x8x8 slice. The times are simulated.
512 devices in a mesh: rep: 8 (over z_hi, core), row: 8 (over z_lo, x), col: 8 (over y).
Axes of the slice: x: 4, y: 8, z: 8 (z_hi: 4, z_lo: 2; z = z_hi * 2 + z_lo), core: 2. Of those that a mesh axis runs over, the one named last changes fastest.
Arguments:
- inputs: bfloat16 [8, 128, 6144], P('rep', 'col', 'row'), may hold values from -6 to 6
- w_in: bfloat16 [6144, 24576], P('row', ('rep', 'col')), may hold values from -0.078125 to 0.078125
- w_out: bfloat16 [24576, 6144], P(('rep', 'col'), 'row'), may hold values from -0.0390625 to 0.0390625
- cotangent: bfloat16 [8, 128, 6144], P('rep', 'col', 'row'), may hold values from -3072 to 3072
- counts: int32 [8], replicated, may hold values from 0 to 4, as said below
Outputs:
- block_output: bfloat16 [8, 128, 6144], P('rep', 'col', 'row')
- input_grad: bfloat16 [8, 128, 6144], P('rep', 'col', 'row')
- w_in_grad: float32 [6144, 24576], P('row', ('rep', 'col'))
- w_out_grad: float32 [24576, 6144], P(('rep', 'col'), 'row')
Inputs may be any that keep to these rules, and one draw needn't show every extreme that they name: Replica r completed its first counts[r] micro-batches; at least one replica completed all 4.
All inputs are finite; a program needn't handle non-finite values.
Results may differ from a plain program's by a relative error of at most 0.015.
Values may be sent and summed in bfloat16 or wider, within the bound.
No kernel may reach another device: no remote copies, remote signals or barrier semaphores. Data moves between devices by JAX's collectives and lax.ppermute only.
A program may use at most 64 MiB of HBM per device.

v0:
```python
import jax
import jax.numpy as jnp
from jax import lax
from jax.sharding import PartitionSpec as P

MBT = 32
root_coef = 0.7978845608028654
cubic_coef = 0.044715


def in_one_piece(arrays, axis, dim, along):
    both = jnp.concatenate(arrays, axis=along)
    result, at, finished = (lax.all_gather(both, axis, axis=dim, tiled=True), 0, [])
    for a in arrays:
        finished.append(lax.slice_in_dim(result, at, at + a.shape[along], axis=along))
        at += a.shape[along]
    return tuple(finished)


def split_up(value, dim, size):
    dims = value.shape
    pieces = value.reshape(*dims[:dim], size, dims[dim] // size, *dims[dim + 1 :])
    return jnp.moveaxis(pieces, dim, 0)


def summed_on_arrival(value, axis, dim):
    size = lax.axis_size(axis)
    pieces = lax.all_to_all(split_up(value, dim, size), axis, 0, 0, tiled=True)
    return jnp.sum(pieces.astype(jnp.float32), axis=0)


def sent_to_all(value, axis):
    size = lax.axis_size(axis)
    return lax.all_to_all(
        jnp.broadcast_to(value[None], (size, *value.shape)), axis, 0, 0, tiled=True
    )


def joined_along(pieces, dim):
    pieces = jnp.moveaxis(pieces, 0, dim)
    dims = pieces.shape
    return pieces.reshape(*dims[:dim], dims[dim] * dims[dim + 1], *dims[dim + 2 :])


def gathered_copies(value, axis, dim):
    pieces = sent_to_all(value, axis)
    return joined_along(pieces, dim)


def gelu_tanh(values):
    inner = root_coef * (values + cubic_coef * values * values * values)
    return 0.5 * values * (1.0 + jnp.tanh(inner))


def gelu_slope(values):
    inner = root_coef * (values + cubic_coef * values * values * values)
    tangent = jnp.tanh(inner)
    return 0.5 * (1.0 + tangent) + 0.5 * values * (1.0 - tangent * tangent) * root_coef * (
        1.0 + 3.0 * cubic_coef * values * values
    )


def right_product(left, right):
    return lax.dot_general(
        left, right, (((1,), (1,)), ((), ())), preferred_element_type=jnp.float32
    )


def first_product(left, right):
    return lax.dot_general(
        left, right, (((0,), (0,)), ((), ())), preferred_element_type=jnp.float32
    )


def body(inputs, w_in, w_out, cotangent, counts):
    rows_local = inputs.shape[1]
    width_local = inputs.shape[2]
    tokens_local = inputs.reshape(rows_local, width_local)
    replicas = lax.axis_size("rep")
    replica_index = lax.axis_index("rep")
    column_index = lax.axis_index("col")
    own_count = jnp.sum(jnp.where(jnp.arange(replicas) == replica_index, counts, 0))
    token_total = (MBT * jnp.sum(counts)).astype(jnp.float32)
    positions = column_index * rows_local + jnp.arange(rows_local, dtype=jnp.int32)
    kept_mask = (positions // MBT < own_count).astype(jnp.float32)
    scaled = (
        cotangent.reshape(rows_local, width_local).astype(jnp.float32)
        * kept_mask[:, None]
        / token_total
    ).astype(jnp.bfloat16)
    tokens_all, scaled_all = in_one_piece((tokens_local, scaled), "col", 0, 1)
    inner_cols = lax.all_gather(w_in, "rep", axis=1, tiled=True)
    outer_rows = lax.all_gather(w_out, "rep", axis=0, tiled=True)
    partial_hidden = jnp.dot(tokens_all, inner_cols, preferred_element_type=jnp.float32)
    hidden = summed_on_arrival(partial_hidden.astype(jnp.bfloat16), "row", 0)
    active_share = gelu_tanh(hidden).astype(jnp.bfloat16)
    activated = gathered_copies(active_share, "row", 0)
    output_terms = jnp.dot(activated, outer_rows, preferred_element_type=jnp.float32)
    output_local = summed_on_arrival(output_terms.astype(jnp.bfloat16), "col", 0)
    block_output = (tokens_local.astype(jnp.float32) + output_local).astype(jnp.bfloat16)
    slope_terms = right_product(scaled_all, outer_rows)
    slope_sum = summed_on_arrival(slope_terms.astype(jnp.bfloat16), "row", 0)
    grad_share = (slope_sum * gelu_slope(hidden)).astype(jnp.bfloat16)
    hidden_grad = gathered_copies(grad_share, "row", 0)
    back_terms = right_product(hidden_grad, inner_cols)
    back_local = summed_on_arrival(back_terms.astype(jnp.bfloat16), "col", 0)
    input_grad = (scaled.astype(jnp.float32) + back_local).astype(jnp.bfloat16)
    token_reps, scaled_reps = in_one_piece((tokens_all, scaled_all), "rep", 0, 1)
    hidden_reps, active_reps = (
        lax.all_to_all(hidden_grad, "rep", split_axis=1, concat_axis=0, tiled=True),
        lax.all_to_all(activated, "rep", split_axis=1, concat_axis=0, tiled=True),
    )
    w_in_grad = first_product(token_reps, hidden_reps)
    w_out_grad = first_product(active_reps, scaled_reps)
    return (
        block_output.reshape(1, rows_local, width_local),
        input_grad.reshape(1, rows_local, width_local),
        w_in_grad,
        w_out_grad,
    )


def solution(mesh):
    placed = (
        P("rep", "col", "row"),
        P("row", ("rep", "col")),
        P(("rep", "col"), "row"),
        P("rep", "col", "row"),
        P(),
    )
    return jax.shard_map(
        body,
        mesh=mesh,
        in_specs=placed,
        out_specs=(
            P("rep", "col", "row"),
            P("rep", "col", "row"),
            P("row", ("rep", "col")),
            P(("rep", "col"), "row"),
        ),
        check_vma=False,
    )
```

profile of v0, /device:TPU:2, one launch (start us, length us, event | category | flops | bytes accessed | tf_op | source)
XLA Modules:
  0.0 305.8 jit_solution(1008410382800476033)
XLA Ops:
  8.7 1.3 fusion.20
  11.3 0.8 fusion.15
  12.1 0.7 pad_maximum_fusion
  12.8 26.6 %all_gather.12 = bf16[128,1536]{1,0:T(8,128)(2,1)S(1)} all-gather(bf16[16,1536]{1,0:T(8,128)(2,1)S(1)} %pad_maximum_fusion), channel_id=1, replica_groups=mesh['rep'=8,'row'=8,'col'=8] {'col'}, dimensions={0}, use_global_device_ids=true | all-gather | bytes 442368 | tf_op jit(solution)/shard_map/all_gather | solution.py:13
  39.4 35.9 %all-gather.6.cloned.1.call-done = bf16[3072,768]{1,0:T(8,128)(2,1)} async-done(((bf16[384,768]{1,0:T(8,128)(2,1)}), bf16[3072,768]{1,0:T(8,128)(2,1)}) %all-gather.6.cloned.1.call-update) | async-done | bytes 4718608 | tf_op jit(solution)/shard_map/all_gather | solution.py:93
  75.3 4.9 %convolution_convert_fusion = bf16[128,3072]{1,0:T(8,128)(2,1)} fusion(bf16[3072,768]{1,0:T(8,128)(2,1)} %all-gather.6.cloned.1.call-done, bf16[128,1536]{1,0:T(8,128)(2,1)S(1)} %all_gather.12), kind=kOutput, calls=%fused_computation | convolution fusion | flops 604372992 | bytes 5701632 | tf_op jit(solution)/shard_map/dot_general | solution.py:64
  80.2 4.8 %all-to-all-start.3 = ((bf16[8,16,3072]{2,1,0:T(8,128)(2,1)}), bf16[8,16,3072]{2,1,0:T(8,128)(2,1)S(1)}, u32[]{:S(2)}, u32[]{:S(2)}) async-start(bf16[8,16,3072]{2,1,0:T(8,128)(2,1)} %bitcast.6), calls=%async_computation.3 | async-start | bytes 1572864 | tf_op jit(solution)/shard_map/all_to_all | solution.py:28
  85.0 53.2 %all-gather.4.cloned.1.call-done = bf16[768,3072]{1,0:T(8,128)(2,1)} async-done(((bf16[768,384]{1,0:T(8,128)(2,1)}), bf16[768,3072]{1,0:T(8,128)(2,1)}) %all-gather.4.cloned.1.call-update) | async-done | bytes 4718608 | tf_op jit(solution)/shard_map/all_gather | solution.py:92
  138.2 4.1 %convolution_convert_fusion.1 = bf16[128,3072]{1,0:T(8,128)(2,1)} fusion(bf16[768,3072]{1,0:T(8,128)(2,1)} %all-gather.4.cloned.1.call-done, bf16[128,1536]{1,0:T(8,128)(2,1)S(1)} %all_gather.12), kind=kOutput, calls=%fused_computation.1 | convolution fusion | flops 604372992 | bytes 5701632 | tf_op jit(solution)/shard_map/dot_general | solution.py:94
  142.3 4.8 %all-to-all-start = ((bf16[8,16,3072]{2,1,0:T(8,128)(2,1)}), bf16[8,16,3072]{2,1,0:T(8,128)(2,1)S(1)}, u32[]{:S(2)}, u32[]{:S(2)}) async-start(bf16[8,16,3072]{2,1,0:T(8,128)(2,1)} %bitcast.2), calls=%async_computation | async-start | bytes 1572864 | tf_op jit(solution)/shard_map/all_to_all | solution.py:28
  147.2 11.1 %all-to-all-done = bf16[8,16,3072]{2,1,0:T(8,128)(2,1)S(1)} async-done(((bf16[8,16,3072]{2,1,0:T(8,128)(2,1)}), bf16[8,16,3072]{2,1,0:T(8,128)(2,1)S(1)}, u32[]{:S(2)}, u32[]{:S(2)}) %all-to-all-start) | async-done | bytes 786464 | tf_op jit(solution)/shard_map/all_to_all | solution.py:28
  158.6 1.0 broadcast_in_dim.9
  159.6 4.8 %all-to-all-start.1 = ((bf16[8,16,3072]{2,1,0:T(8,128)(2,1)}), bf16[8,16,3072]{2,1,0:T(8,128)(2,1)S(1)}, u32[]{:S(2)}, u32[]{:S(2)}) async-start(bf16[8,16,3072]{2,1,0:T(8,128)(2,1)} %broadcast_in_dim.9), calls=%async_computation.1 | async-start | bytes 1572864 | tf_op jit(solution)/shard_map/all_to_all | solution.py:34
  164.4 0.7 all-gather.8.cloned.1.call-update
  165.1 10.3 %all-to-all-done.1 = bf16[8,16,3072]{2,1,0:T(8,128)(2,1)S(1)} async-done(((bf16[8,16,3072]{2,1,0:T(8,128)(2,1)}), bf16[8,16,3072]{2,1,0:T(8,128)(2,1)S(1)}, u32[]{:S(2)}, u32[]{:S(2)}) %all-to-all-start.1) | async-done | bytes 786464 | tf_op jit(solution)/shard_map/all_to_all | solution.py:34
  175.4 1.0 broadcast_in_dim.10
  176.3 4.8 %all-to-all-start.4 = ((bf16[8,16,3072]{2,1,0:T(8,128)(2,1)}), bf16[8,16,3072]{2,1,0:T(8,128)(2,1)S(1)}, u32[]{:S(2)}, u32[]{:S(2)}) async-start(bf16[8,16,3072]{2,1,0:T(8,128)(2,1)} %broadcast_in_dim.10), calls=%async_computation.4 | async-start | bytes 1572864 | tf_op jit(solution)/shard_map/all_to_all | solution.py:34
  181.2 3.8 %convolution_convert_fusion.3 = bf16[128,768]{1,0:T(8,128)(2,1)} fusion(bf16[128,3072]{1,0:T(8,128)(2,1)S(1)} %bitcast.43, bf16[3072,768]{1,0:T(8,128)(2,1)} %all-gather.6.cloned.1.call-done), kind=kOutput, calls=%fused_computation.9 | convolution fusion | flops 604078080 | bytes 5701632 | tf_op jit(solution)/shard_map/dot_general | solution.py:98
  185.0 26.9 %all-to-all-done.4 = bf16[8,16,3072]{2,1,0:T(8,128)(2,1)S(1)} async-done(((bf16[8,16,3072]{2,1,0:T(8,128)(2,1)}), bf16[8,16,3072]{2,1,0:T(8,128)(2,1)S(1)}, u32[]{:S(2)}, u32[]{:S(2)}) %all-to-all-start.4) | async-done | bytes 786464 | tf_op jit(solution)/shard_map/all_to_all | solution.py:34
  211.9 6.9 %all-to-all-start.2 = ((bf16[8,16,768]{2,1,0:T(8,128)(2,1)}), bf16[8,16,768]{2,1,0:T(8,128)(2,1)S(1)}, u32[]{:S(2)}, u32[]{:S(2)}) async-start(bf16[8,16,768]{2,1,0:T(8,128)(2,1)} %bitcast.4), calls=%async_computation.2 | async-start | bytes 393216 | tf_op jit(solution)/shard_map/all_to_all | solution.py:28
  218.8 4.7 %convolution_convert_fusion.2 = bf16[128,768]{1,0:T(8,128)(2,1)} fusion(bf16[128,3072]{1,0:T(8,128)(2,1)S(1)} %bitcast.45, bf16[768,3072]{1,0:T(8,128)(2,1)} %all-gather.4.cloned.1.call-done), kind=kOutput, calls=%fused_computation.8 | convolution fusion | flops 604078080 | bytes 5701632 | tf_op jit(solution)/shard_map/dot_general | solution.py:64
  223.5 5.3 %all-to-all-done.2 = bf16[8,16,768]{2,1,0:T(8,128)(2,1)S(1)} async-done(((bf16[8,16,768]{2,1,0:T(8,128)(2,1)}), bf16[8,16,768]{2,1,0:T(8,128)(2,1)S(1)}, u32[]{:S(2)}, u32[]{:S(2)}) %all-to-all-start.2) | async-done | bytes 196640 | tf_op jit(solution)/shard_map/all_to_all | solution.py:28
  228.7 3.4 %all-to-all-start.5 = ((bf16[8,16,768]{2,1,0:T(8,128)(2,1)}), bf16[8,16,768]{2,1,0:T(8,128)(2,1)S(1)}, u32[]{:S(2)}, u32[]{:S(2)}) async-start(bf16[8,16,768]{2,1,0:T(8,128)(2,1)} %bitcast.8), calls=%async_computation.5 | async-start | bytes 393216 | tf_op jit(solution)/shard_map/all_to_all | solution.py:28
  232.3 1.0 copy.11
  233.3 8.6 %all-to-all-done.5 = bf16[8,16,768]{2,1,0:T(8,128)(2,1)S(1)} async-done(((bf16[8,16,768]{2,1,0:T(8,128)(2,1)}), bf16[8,16,768]{2,1,0:T(8,128)(2,1)S(1)}, u32[]{:S(2)}, u32[]{:S(2)}) %all-to-all-start.5) | async-done | bytes 196640 | tf_op jit(solution)/shard_map/all_to_all | solution.py:28
  241.8 3.5 %all-to-all-start.6 = ((bf16[128,8,384]{2,0,1:T(8,128)(2,1)}), bf16[128,8,384]{2,0,1:T(8,128)(2,1)S(1)}, u32[]{:S(2)}, u32[]{:S(2)}) async-start(bf16[128,8,384]{2,0,1:T(8,128)(2,1)} %copy.11), calls=%async_computation.6 | async-start | bytes 1572864 | tf_op jit(solution)/shard_map/all_to_all | solution.py:110
  245.5 1.0 copy.12
  246.5 22.3 %all-to-all-done.6 = bf16[128,8,384]{2,0,1:T(8,128)(2,1)S(1)} async-done(((bf16[128,8,384]{2,0,1:T(8,128)(2,1)}), bf16[128,8,384]{2,0,1:T(8,128)(2,1)S(1)}, u32[]{:S(2)}, u32[]{:S(2)}) %all-to-all-start.6) | async-done | bytes 786464 | tf_op jit(solution)/shard_map/all_to_all | solution.py:110
  268.8 3.5 %all-to-all-start.7 = ((bf16[128,8,384]{2,0,1:T(8,128)(2,1)}), bf16[128,8,384]{2,0,1:T(8,128)(2,1)S(1)}, u32[]{:S(2)}, u32[]{:S(2)}) async-start(bf16[128,8,384]{2,0,1:T(8,128)(2,1)} %copy.12), calls=%async_computation.7 | async-start | bytes 1572864 | tf_op jit(solution)/shard_map/all_to_all | solution.py:111
  273.8 3.4 %fusion.2 = f32[768,384]{1,0:T(8,128)} fusion(bf16[1024,384]{1,0:T(8,128)(2,1)S(1)} %bitcast.49, bf16[1024,1536]{1,0:T(8,128)(2,1)} %all-gather.8.cloned.1.call-done), kind=kOutput, calls=%fused_computation.4 | convolution fusion | flops 603979776 | bytes 3538944 | tf_op jit(solution)/shard_map/dot_general | solution.py:70
  277.2 18.9 %all-to-all-done.7 = bf16[128,8,384]{2,0,1:T(8,128)(2,1)S(1)} async-done(((bf16[128,8,384]{2,0,1:T(8,128)(2,1)}), bf16[128,8,384]{2,0,1:T(8,128)(2,1)S(1)}, u32[]{:S(2)}, u32[]{:S(2)}) %all-to-all-start.7) | async-done | bytes 786464 | tf_op jit(solution)/shard_map/all_to_all | solution.py:111
  296.1 3.2 %fusion = f32[384,768]{1,0:T(8,128)} fusion(bf16[1024,384]{1,0:T(8,128)(2,1)S(1)} %bitcast.50, bf16[1024,1536]{1,0:T(8,128)(2,1)} %all-gather.8.cloned.1.call-done), kind=kOutput, calls=%fused_computation.2 | convolution fusion | flops 603979776 | bytes 3538944 | tf_op jit(solution)/shard_map/dot_general | solution.py:70
  (23 shorter events, 4.1 us)
Async XLA Ops:
  7.2 68.2 %all-gather.6.cloned.1.call-start = ((), (), s32[]{:S(2)}) async-start(), calls=%async_computation.9 | async-start | bytes 5308416 | tf_op jit(solution)/shard_map/all_gather | solution.py:93
  7.9 130.3 %all-gather.4.cloned.1.call-start = ((), (), s32[]{:S(2)}) async-start(), calls=%async_computation.8 | async-start | bytes 5308416 | tf_op jit(solution)/shard_map/all_gather | solution.py:92
  39.4 98.8 %copy-start = (bf16[128,1536]{1,0:T(8,128)(2,1)}, bf16[128,1536]{1,0:T(8,128)(2,1)S(1)}, u32[]{:S(2)}) copy-start(bf16[128,1536]{1,0:T(8,128)(2,1)S(1)} %all_gather.12) | copy-start | bytes 1179652
  80.2 62.1 %all-to-all-start.3 = ((bf16[8,16,3072]{2,1,0:T(8,128)(2,1)}), bf16[8,16,3072]{2,1,0:T(8,128)(2,1)S(1)}, u32[]{:S(2)}, u32[]{:S(2)}) async-start(bf16[8,16,3072]{2,1,0:T(8,128)(2,1)} %bitcast.6), calls=%async_computation.3 | async-start | bytes 1572864 | tf_op jit(solution)/shard_map/all_to_all | solution.py:28
  142.3 16.1 %all-to-all-start = ((bf16[8,16,3072]{2,1,0:T(8,128)(2,1)}), bf16[8,16,3072]{2,1,0:T(8,128)(2,1)S(1)}, u32[]{:S(2)}, u32[]{:S(2)}) async-start(bf16[8,16,3072]{2,1,0:T(8,128)(2,1)} %bitcast.2), calls=%async_computation | async-start | bytes 1572864 | tf_op jit(solution)/shard_map/all_to_all | solution.py:28
  159.6 15.8 %all-to-all-start.1 = ((bf16[8,16,3072]{2,1,0:T(8,128)(2,1)}), bf16[8,16,3072]{2,1,0:T(8,128)(2,1)S(1)}, u32[]{:S(2)}, u32[]{:S(2)}) async-start(bf16[8,16,3072]{2,1,0:T(8,128)(2,1)} %broadcast_in_dim.9), calls=%async_computation.1 | async-start | bytes 1572864 | tf_op jit(solution)/shard_map/all_to_all | solution.py:34
  164.4 109.4 %all-gather.8.cloned.1.call-start = ((), (), s32[]{:S(2)}) async-start(), calls=%async_computation.10 | async-start | bytes 3538944 | tf_op jit(solution)/shard_map/all_gather | solution.py:13
  176.3 35.5 %all-to-all-start.4 = ((bf16[8,16,3072]{2,1,0:T(8,128)(2,1)}), bf16[8,16,3072]{2,1,0:T(8,128)(2,1)S(1)}, u32[]{:S(2)}, u32[]{:S(2)}) async-start(bf16[8,16,3072]{2,1,0:T(8,128)(2,1)} %broadcast_in_dim.10), calls=%async_computation.4 | async-start | bytes 1572864 | tf_op jit(solution)/shard_map/all_to_all | solution.py:34
  211.9 16.9 %all-to-all-start.2 = ((bf16[8,16,768]{2,1,0:T(8,128)(2,1)}), bf16[8,16,768]{2,1,0:T(8,128)(2,1)S(1)}, u32[]{:S(2)}, u32[]{:S(2)}) async-start(bf16[8,16,768]{2,1,0:T(8,128)(2,1)} %bitcast.4), calls=%async_computation.2 | async-start | bytes 393216 | tf_op jit(solution)/shard_map/all_to_all | solution.py:28
  228.7 13.1 %all-to-all-start.5 = ((bf16[8,16,768]{2,1,0:T(8,128)(2,1)}), bf16[8,16,768]{2,1,0:T(8,128)(2,1)S(1)}, u32[]{:S(2)}, u32[]{:S(2)}) async-start(bf16[8,16,768]{2,1,0:T(8,128)(2,1)} %bitcast.8), calls=%async_computation.5 | async-start | bytes 393216 | tf_op jit(solution)/shard_map/all_to_all | solution.py:28
  233.3 39.2 %copy-start.2 = (bf16[1,16,768]{2,1,0:T(8,128)(2,1)S(1)}, bf16[1,16,768]{2,1,0:T(8,128)(2,1)}, u32[]{:S(2)}) copy-start(bf16[1,16,768]{2,1,0:T(8,128)(2,1)} %param.5) | copy-start | bytes 73732
  233.3 39.8 %copy-start.1 = (bf16[1,16,768]{2,1,0:T(8,128)(2,1)S(1)}, bf16[1,16,768]{2,1,0:T(8,128)(2,1)}, u32[]{:S(2)}) copy-start(bf16[1,16,768]{2,1,0:T(8,128)(2,1)} %param.8) | copy-start | bytes 73732
  241.8 27.0 %all-to-all-start.6 = ((bf16[128,8,384]{2,0,1:T(8,128)(2,1)}), bf16[128,8,384]{2,0,1:T(8,128)(2,1)S(1)}, u32[]{:S(2)}, u32[]{:S(2)}) async-start(bf16[128,8,384]{2,0,1:T(8,128)(2,1)} %copy.11), calls=%async_computation.6 | async-start | bytes 1572864 | tf_op jit(solution)/shard_map/all_to_all | solution.py:110
  268.8 27.3 %all-to-all-start.7 = ((bf16[128,8,384]{2,0,1:T(8,128)(2,1)}), bf16[128,8,384]{2,0,1:T(8,128)(2,1)S(1)}, u32[]{:S(2)}, u32[]{:S(2)}) async-start(bf16[128,8,384]{2,0,1:T(8,128)(2,1)} %copy.12), calls=%async_computation.7 | async-start | bytes 1572864 | tf_op jit(solution)/shard_map/all_to_all | solution.py:111
Sparse Core Ops, SparseCore 0:
  10.1 65.1 all-gather.5
  77.5 60.7 all-gather.3
  167.3 52.0 all-gather.7
where the time goes:
time: 307 us; the launch traced here: 306 us
  waiting for transfers between devices  195 us (64%)
  starting transfers between devices  36.7 us (12%)
  blocking collectives  26.6 us (9%)
  matrix products  24.1 us (8%)
  between operations  14.5 us (5%)
  other arithmetic  5.26 us (2%)
  local copies, waits for them, and re-layouts  4.15 us (1%)
    all_gather x1, waiting for transfers between devices, body(): inner_cols = lax.all_gather(w_in, 'rep', axis=1, tiled=True)  53.2 us
    all_to_all x2, waiting for transfers between devices, sent_to_all(): lax.all_to_all(jnp.broadcast_to(value[None], (size, *value.shape)), axis,...  37.2 us
    all_gather x1, waiting for transfers between devices, body(): outer_rows = lax.all_gather(w_out, 'rep', axis=0, tiled=True)  35.9 us
    all_gather x1, blocking collectives, in_one_piece(): lax.all_gather(both, axis, axis=dim, tiled=True)  26.6 us
    all_to_all x4, waiting for transfers between devices, summed_on_arrival(): pieces = lax.all_to_all(split_up(value, dim, size), axis, 0, 0, tiled=True)  25 us
    all_to_all x1, waiting for transfers between devices, body(): lax.all_to_all(hidden_grad, 'rep', split_axis=1, concat_axis=0, tiled=True)  22.3 us
    all_to_all x4, starting transfers between devices, summed_on_arrival(): pieces = lax.all_to_all(split_up(value, dim, size), axis, 0, 0, tiled=True)  19.9 us
    all_to_all x1, waiting for transfers between devices, body(): lax.all_to_all(activated, 'rep', split_axis=1, concat_axis=0, tiled=True)  18.9 us
  transfers between devices with their start and end apart: 11, of which 9 were waited for; matrix products, arithmetic and copies ran while one was open for 10% of the time, Pallas kernels for 0%

commit v1 on v0

--- a/solution.py
+++ b/solution.py
@@ -6,6 +6,12 @@
 MBT = 32
 root_coef = 0.7978845608028654
 cubic_coef = 0.044715
+
+
+def swap_blocks(value, name, split, join):
+    parts = jnp.split(value, lax.axis_size(name), axis=split)
+    received = lax.all_to_all(jnp.stack(parts), name, 0, 0)
+    return jnp.concatenate(received, axis=join)
 
 
 def in_one_piece(arrays, axis, dim, along):
@@ -107,7 +113,7 @@
     input_grad = (scaled.astype(jnp.float32) + back_local).astype(jnp.bfloat16)
     token_reps, scaled_reps = in_one_piece((tokens_all, scaled_all), "rep", 0, 1)
     hidden_reps, active_reps = (
-        lax.all_to_all(hidden_grad, "rep", split_axis=1, concat_axis=0, tiled=True),
+        swap_blocks(hidden_grad, "rep", 1, 0),
         lax.all_to_all(activated, "rep", split_axis=1, concat_axis=0, tiled=True),
     )
     w_in_grad = first_product(token_reps, hidden_reps)

time: 307 us -> 288 us (0.938)
  the two profiles are of different devices: /device:TPU:2 before, /device:TPU:8 now
where the time goes in v1:
time: 288 us; the launch traced here: 287 us
  waiting for transfers between devices  158 us (55%)
  blocking collectives  44.3 us (15%)
  starting transfers between devices  34 us (12%)
  matrix products  24.1 us (8%)
  between operations  14.5 us (5%)
  local copies, waits for them, and re-layouts  7.34 us (3%)
  other arithmetic  5.26 us (2%)
    all_gather x1, waiting for transfers between devices, body(): inner_cols = lax.all_gather(w_in, 'rep', axis=1, tiled=True)  53.8 us
    all_gather x1, waiting for transfers between devices, body(): outer_rows = lax.all_gather(w_out, 'rep', axis=0, tiled=True)  34.7 us
    all_gather x1, blocking collectives, in_one_piece(): lax.all_gather(both, axis, axis=dim, tiled=True)  27.8 us
    all_to_all x4, starting transfers between devices, summed_on_arrival(): pieces = lax.all_to_all(split_up(value, dim, size), axis, 0, 0, tiled=True)  23 us
    all_to_all x1, waiting for transfers between devices, swap_blocks(): received = lax.all_to_all(jnp.stack(parts), name, 0, 0)  22.6 us
    all_to_all x4, waiting for transfers between devices, summed_on_arrival(): pieces = lax.all_to_all(split_up(value, dim, size), axis, 0, 0, tiled=True)  19.3 us
    all_to_all x1, waiting for transfers between devices, body(): lax.all_to_all(activated, 'rep', split_axis=1, concat_axis=0, tiled=True)  18.8 us
    all_to_all x1, blocking collectives, sent_to_all(): lax.all_to_all(jnp.broadcast_to(value[None], (size, *value.shape)), axis,...  16.5 us
  transfers between devices with their start and end apart: 10, of which 7 were waited for; matrix products, arithmetic and copies ran while one was open for 11% of the time, Pallas kernels for 0%

profile of v1, /device:TPU:8, one launch (start us, length us, event | category | flops | bytes accessed | tf_op | source)
XLA Modules:
  0.0 287.0 jit_solution(9471991098341842959)
XLA Ops:
  7.2 0.7 all-gather.6.cloned.1.call-update
  7.9 0.7 all-gather.4.cloned.1.call-update
  8.7 1.3 fusion.28
  10.6 0.7 compare_convert_fusion
  11.3 0.8 fusion.23
  12.1 0.7 pad_maximum_fusion
  12.8 27.8 %all_gather.12 = bf16[128,1536]{1,0:T(8,128)(2,1)S(1)} all-gather(bf16[16,1536]{1,0:T(8,128)(2,1)S(1)} %pad_maximum_fusion), channel_id=1, replica_groups=mesh['rep'=8,'row'=8,'col'=8] {'col'}, dimensions={0}, use_global_device_ids=true | all-gather | bytes 442368 | tf_op jit(solution)/shard_map/all_gather | solution.py:19
  40.6 34.7 %all-gather.6.cloned.1.call-done = bf16[3072,768]{1,0:T(8,128)(2,1)} async-done(((bf16[384,768]{1,0:T(8,128)(2,1)}), bf16[3072,768]{1,0:T(8,128)(2,1)}) %all-gather.6.cloned.1.call-update) | async-done | bytes 4718608 | tf_op jit(solution)/shard_map/all_gather | solution.py:99
  75.3 4.9 %convolution_convert_fusion = bf16[128,3072]{1,0:T(8,128)(2,1)} fusion(bf16[3072,768]{1,0:T(8,128)(2,1)} %all-gather.6.cloned.1.call-done, bf16[128,1536]{1,0:T(8,128)(2,1)S(1)} %all_gather.12), kind=kOutput, calls=%fused_computation | convolution fusion | flops 604372992 | bytes 5701632 | tf_op jit(solution)/shard_map/dot_general | solution.py:70
  80.2 4.3 %all-to-all-start.3 = ((bf16[8,16,3072]{2,1,0:T(8,128)(2,1)}), bf16[8,16,3072]{2,1,0:T(8,128)(2,1)S(1)}, u32[]{:S(2)}, u32[]{:S(2)}) async-start(bf16[8,16,3072]{2,1,0:T(8,128)(2,1)} %bitcast.6), calls=%async_computation.3 | async-start | bytes 1572864 | tf_op jit(solution)/shard_map/all_to_all | solution.py:34
  84.4 53.8 %all-gather.4.cloned.1.call-done = bf16[768,3072]{1,0:T(8,128)(2,1)} async-done(((bf16[768,384]{1,0:T(8,128)(2,1)}), bf16[768,3072]{1,0:T(8,128)(2,1)}) %all-gather.4.cloned.1.call-update) | async-done | bytes 4718608 | tf_op jit(solution)/shard_map/all_gather | solution.py:98
  138.2 4.1 %convolution_convert_fusion.1 = bf16[128,3072]{1,0:T(8,128)(2,1)} fusion(bf16[768,3072]{1,0:T(8,128)(2,1)} %all-gather.4.cloned.1.call-done, bf16[128,1536]{1,0:T(8,128)(2,1)S(1)} %all_gather.12), kind=kOutput, calls=%fused_computation.1 | convolution fusion | flops 604372992 | bytes 5701632 | tf_op jit(solution)/shard_map/dot_general | solution.py:100
  142.3 4.2 %all-to-all-start = ((bf16[8,16,3072]{2,1,0:T(8,128)(2,1)}), bf16[8,16,3072]{2,1,0:T(8,128)(2,1)S(1)}, u32[]{:S(2)}, u32[]{:S(2)}) async-start(bf16[8,16,3072]{2,1,0:T(8,128)(2,1)} %bitcast.2), calls=%async_computation | async-start | bytes 1572864 | tf_op jit(solution)/shard_map/all_to_all | solution.py:34
  146.6 12.3 %all-to-all-done = bf16[8,16,3072]{2,1,0:T(8,128)(2,1)S(1)} async-done(((bf16[8,16,3072]{2,1,0:T(8,128)(2,1)}), bf16[8,16,3072]{2,1,0:T(8,128)(2,1)S(1)}, u32[]{:S(2)}, u32[]{:S(2)}) %all-to-all-start) | async-done | bytes 786464 | tf_op jit(solution)/shard_map/all_to_all | solution.py:34
  159.3 16.5 %all_to_all.54 = bf16[8,16,3072]{2,1,0:T(8,128)(2,1)S(1)} all-to-all(bf16[8,16,3072]{2,1,0:T(8,128)(2,1)S(1)} %broadcast_in_dim.9), channel_id=1, replica_groups=mesh['rep'=8,'row'=8,'col'=8] {'row'}, dimensions={0} | all-to-all | bytes 1572864 | tf_op jit(solution)/shard_map/all_to_all | solution.py:40
  175.8 1.0 broadcast_in_dim.10
  176.7 3.5 %all-to-all-start.4 = ((bf16[8,16,3072]{2,1,0:T(8,128)(2,1)}), bf16[8,16,3072]{2,1,0:T(8,128)(2,1)S(1)}, u32[]{:S(2)}, u32[]{:S(2)}) async-start(bf16[8,16,3072]{2,1,0:T(8,128)(2,1)} %broadcast_in_dim.10), calls=%async_computation.4 | async-start | bytes 1572864 | tf_op jit(solution)/shard_map/all_to_all | solution.py:40
  180.4 0.7 all-gather.8.cloned.1.call-update
  181.0 3.8 %convolution_convert_fusion.3 = bf16[128,768]{1,0:T(8,128)(2,1)} fusion(bf16[128,3072]{1,0:T(8,128)(2,1)S(1)} %bitcast.70, bf16[3072,768]{1,0:T(8,128)(2,1)} %all-gather.6.cloned.1.call-done), kind=kOutput, calls=%fused_computation.9 | convolution fusion | flops 604078080 | bytes 5701632 | tf_op jit(solution)/shard_map/dot_general | solution.py:104
  184.9 6.3 %all-to-all-done.4 = bf16[8,16,3072]{2,1,0:T(8,128)(2,1)S(1)} async-done(((bf16[8,16,3072]{2,1,0:T(8,128)(2,1)}), bf16[8,16,3072]{2,1,0:T(8,128)(2,1)S(1)}, u32[]{:S(2)}, u32[]{:S(2)}) %all-to-all-start.4) | async-done | bytes 786464 | tf_op jit(solution)/shard_map/all_to_all | solution.py:40
  191.2 7.3 %all-to-all-start.2 = ((bf16[8,16,768]{2,1,0:T(8,128)(2,1)}), bf16[8,16,768]{2,1,0:T(8,128)(2,1)S(1)}, u32[]{:S(2)}, u32[]{:S(2)}) async-start(bf16[8,16,768]{2,1,0:T(8,128)(2,1)} %bitcast.4), calls=%async_computation.2 | async-start | bytes 393216 | tf_op jit(solution)/shard_map/all_to_all | solution.py:34
  202.4 4.7 %convolution_convert_fusion.2 = bf16[128,768]{1,0:T(8,128)(2,1)} fusion(bf16[128,3072]{1,0:T(8,128)(2,1)S(1)} %bitcast.78, bf16[768,3072]{1,0:T(8,128)(2,1)} %all-gather.4.cloned.1.call-done), kind=kOutput, calls=%fused_computation.8 | convolution fusion | flops 604078080 | bytes 5701632 | tf_op jit(solution)/shard_map/dot_general | solution.py:70
  207.1 7.2 %all-to-all-start.5 = ((bf16[8,16,768]{2,1,0:T(8,128)(2,1)}), bf16[8,16,768]{2,1,0:T(8,128)(2,1)S(1)}, u32[]{:S(2)}, u32[]{:S(2)}) async-start(bf16[8,16,768]{2,1,0:T(8,128)(2,1)} %bitcast.8), calls=%async_computation.5 | async-start | bytes 393216 | tf_op jit(solution)/shard_map/all_to_all | solution.py:34
  215.6 7.0 %all-to-all-done.5 = bf16[8,16,768]{2,1,0:T(8,128)(2,1)S(1)} async-done(((bf16[8,16,768]{2,1,0:T(8,128)(2,1)}), bf16[8,16,768]{2,1,0:T(8,128)(2,1)S(1)}, u32[]{:S(2)}, u32[]{:S(2)}) %all-to-all-start.5) | async-done | bytes 196640 | tf_op jit(solution)/shard_map/all_to_all | solution.py:34
  222.6 3.8 %all-to-all-start.6 = ((bf16[8,128,384]{2,1,0:T(8,128)(2,1)}), bf16[8,128,384]{2,1,0:T(8,128)(2,1)S(1)}, u32[]{:S(2)}, u32[]{:S(2)}) async-start(bf16[8,128,384]{2,1,0:T(8,128)(2,1)} %fusion.13), calls=%async_computation.6 | async-start | bytes 1572864 | tf_op jit(solution)/shard_map/all_to_all | solution.py:13
  226.6 1.0 copy.10
  227.5 22.6 %all-to-all-done.6 = bf16[8,128,384]{2,1,0:T(8,128)(2,1)S(1)} async-done(((bf16[8,128,384]{2,1,0:T(8,128)(2,1)}), bf16[8,128,384]{2,1,0:T(8,128)(2,1)S(1)}, u32[]{:S(2)}, u32[]{:S(2)}) %all-to-all-start.6) | async-done | bytes 786464 | tf_op jit(solution)/shard_map/all_to_all | solution.py:13
  250.1 3.5 %all-to-all-start.7 = ((bf16[128,8,384]{2,0,1:T(8,128)(2,1)}), bf16[128,8,384]{2,0,1:T(8,128)(2,1)S(1)}, u32[]{:S(2)}, u32[]{:S(2)}) async-start(bf16[128,8,384]{2,0,1:T(8,128)(2,1)} %copy.10), calls=%async_computation.7 | async-start | bytes 1572864 | tf_op jit(solution)/shard_map/all_to_all | solution.py:117
  254.4 0.7 fusion.26
  255.1 3.4 %fusion.2 = f32[768,384]{1,0:T(8,128)} fusion(bf16[1024,384]{1,0:T(8,128)(2,1)S(1)} %bitcast.82, bf16[1024,1536]{1,0:T(8,128)(2,1)} %all-gather.8.cloned.1.call-done), kind=kOutput, calls=%fused_computation.4 | convolution fusion | flops 603979776 | bytes 3538944 | tf_op jit(solution)/shard_map/dot_general | solution.py:76
  258.5 18.8 %all-to-all-done.7 = bf16[128,8,384]{2,0,1:T(8,128)(2,1)S(1)} async-done(((bf16[128,8,384]{2,0,1:T(8,128)(2,1)}), bf16[128,8,384]{2,0,1:T(8,128)(2,1)S(1)}, u32[]{:S(2)}, u32[]{:S(2)}) %all-to-all-start.7) | async-done | bytes 786464 | tf_op jit(solution)/shard_map/all_to_all | solution.py:117
  277.3 3.2 %fusion = f32[384,768]{1,0:T(8,128)} fusion(bf16[1024,384]{1,0:T(8,128)(2,1)S(1)} %bitcast.83, bf16[1024,1536]{1,0:T(8,128)(2,1)} %all-gather.8.cloned.1.call-done), kind=kOutput, calls=%fused_computation.2 | convolution fusion | flops 603979776 | bytes 3538944 | tf_op jit(solution)/shard_map/dot_general | solution.py:76
  (28 shorter events, 6.6 us)
Async XLA Ops:
  7.2 68.1 %all-gather.6.cloned.1.call-start = ((), (), s32[]{:S(2)}) async-start(), calls=%async_computation.9 | async-start | bytes 5308416 | tf_op jit(solution)/shard_map/all_gather | solution.py:99
  7.9 130.3 %all-gather.4.cloned.1.call-start = ((), (), s32[]{:S(2)}) async-start(), calls=%async_computation.8 | async-start | bytes 5308416 | tf_op jit(solution)/shard_map/all_gather | solution.py:98
  40.6 97.6 %copy-start = (bf16[128,1536]{1,0:T(8,128)(2,1)}, bf16[128,1536]{1,0:T(8,128)(2,1)S(1)}, u32[]{:S(2)}) copy-start(bf16[128,1536]{1,0:T(8,128)(2,1)S(1)} %all_gather.12) | copy-start | bytes 1179652
  80.2 62.1 %all-to-all-start.3 = ((bf16[8,16,3072]{2,1,0:T(8,128)(2,1)}), bf16[8,16,3072]{2,1,0:T(8,128)(2,1)S(1)}, u32[]{:S(2)}, u32[]{:S(2)}) async-start(bf16[8,16,3072]{2,1,0:T(8,128)(2,1)} %bitcast.6), calls=%async_computation.3 | async-start | bytes 1572864 | tf_op jit(solution)/shard_map/all_to_all | solution.py:34
  142.3 16.6 %all-to-all-start = ((bf16[8,16,3072]{2,1,0:T(8,128)(2,1)}), bf16[8,16,3072]{2,1,0:T(8,128)(2,1)S(1)}, u32[]{:S(2)}, u32[]{:S(2)}) async-start(bf16[8,16,3072]{2,1,0:T(8,128)(2,1)} %bitcast.2), calls=%async_computation | async-start | bytes 1572864 | tf_op jit(solution)/shard_map/all_to_all | solution.py:34
  176.7 14.4 %all-to-all-start.4 = ((bf16[8,16,3072]{2,1,0:T(8,128)(2,1)}), bf16[8,16,3072]{2,1,0:T(8,128)(2,1)S(1)}, u32[]{:S(2)}, u32[]{:S(2)}) async-start(bf16[8,16,3072]{2,1,0:T(8,128)(2,1)} %broadcast_in_dim.10), calls=%async_computation.4 | async-start | bytes 1572864 | tf_op jit(solution)/shard_map/all_to_all | solution.py:40
  180.3 74.8 %all-gather.8.cloned.1.call-start = ((), (), s32[]{:S(2)}) async-start(), calls=%async_computation.10 | async-start | bytes 3538944 | tf_op jit(solution)/shard_map/all_gather | solution.py:19
  191.2 15.9 %all-to-all-start.2 = ((bf16[8,16,768]{2,1,0:T(8,128)(2,1)}), bf16[8,16,768]{2,1,0:T(8,128)(2,1)S(1)}, u32[]{:S(2)}, u32[]{:S(2)}) async-start(bf16[8,16,768]{2,1,0:T(8,128)(2,1)} %bitcast.4), calls=%async_computation.2 | async-start | bytes 393216 | tf_op jit(solution)/shard_map/all_to_all | solution.py:34
  207.1 15.5 %all-to-all-start.5 = ((bf16[8,16,768]{2,1,0:T(8,128)(2,1)}), bf16[8,16,768]{2,1,0:T(8,128)(2,1)S(1)}, u32[]{:S(2)}, u32[]{:S(2)}) async-start(bf16[8,16,768]{2,1,0:T(8,128)(2,1)} %bitcast.8), calls=%async_computation.5 | async-start | bytes 393216 | tf_op jit(solution)/shard_map/all_to_all | solution.py:34
  215.6 38.2 %copy-start.2 = (bf16[1,16,768]{2,1,0:T(8,128)(2,1)S(1)}, bf16[1,16,768]{2,1,0:T(8,128)(2,1)}, u32[]{:S(2)}) copy-start(bf16[1,16,768]{2,1,0:T(8,128)(2,1)} %param.5) | copy-start | bytes 73732
  215.6 38.8 %copy-start.1 = (bf16[1,16,768]{2,1,0:T(8,128)(2,1)S(1)}, bf16[1,16,768]{2,1,0:T(8,128)(2,1)}, u32[]{:S(2)}) copy-start(bf16[1,16,768]{2,1,0:T(8,128)(2,1)} %param.8) | copy-start | bytes 73732
  222.6 27.5 %all-to-all-start.6 = ((bf16[8,128,384]{2,1,0:T(8,128)(2,1)}), bf16[8,128,384]{2,1,0:T(8,128)(2,1)S(1)}, u32[]{:S(2)}, u32[]{:S(2)}) async-start(bf16[8,128,384]{2,1,0:T(8,128)(2,1)} %fusion.13), calls=%async_computation.6 | async-start | bytes 1572864 | tf_op jit(solution)/shard_map/all_to_all | solution.py:13
  250.1 27.1 %all-to-all-start.7 = ((bf16[128,8,384]{2,0,1:T(8,128)(2,1)}), bf16[128,8,384]{2,0,1:T(8,128)(2,1)S(1)}, u32[]{:S(2)}, u32[]{:S(2)}) async-start(bf16[128,8,384]{2,0,1:T(8,128)(2,1)} %copy.10), calls=%async_computation.7 | async-start | bytes 1572864 | tf_op jit(solution)/shard_map/all_to_all | solution.py:117
Sparse Core Ops, SparseCore 0:
  10.1 65.1 all-gather.5
  77.4 60.7 all-gather.3
  183.3 45.8 all-gather.7
